TPU v7x, 128 devices: a whole 4x4x4 slice. The times are simulated.
128 devices in a mesh: space: 32 (over z, y, core), orb: 4 (over x).
Axes of the slice: x: 4, y: 4, z: 4, core: 2. Of those that a mesh axis runs over, the one named last changes fastest.
Arguments:
- orbitals: float32 [8, 32768, 256], P('orb', 'space'), may hold values from -6 to 6
- near_source: int32 [32768, 27], P('space'), may hold values from 0 to 32767, as said below
- far_leaf: int32 [32768, 108], P('space'), may hold values from 0 to 32767, as said below
- far_mid: int32 [4096, 108], P('space'), may hold values from 0 to 4095, as said below
- far_top: int32 [512, 108], P('space'), may hold values from 0 to 511, as said below
- leaf_basis: bfloat16 [64, 256], replicated, may hold values from -0.375 to 0.375
- near_table: bfloat16 [27, 256, 256], replicated, may hold values from -0.078125 to 0.078125
- transfer: bfloat16 [8, 64, 64], replicated, may hold values from -0.75 to 0.75
- coupling: bfloat16 [108, 64, 64], replicated, may hold values from -0.078125 to 0.078125
- pair_transfer: bfloat16 [2, 64, 64], replicated, may hold values from -0.75 to 0.75
- coarse_coupling: bfloat16 [4, 64, 64], replicated, may hold values from -0.4375 to 0.4375
Outputs:
- relaxed: float32 [8, 32768, 256], P('orb', 'space')
Inputs may be any that keep to these rules, and one draw needn't show every extreme that they name: `near_source`: with layer(t) = t // 64: every entry of leaf t lies in a layer at most 1 from layer(t); entry 13 is t itself; entry 0 is the leaf at t's transverse position one layer away. `far_leaf`: with layer(t) = t // 64: every entry of box t lies in a layer 2 or 3 away from layer(t); entry 0 is exactly 3 layers away. `far_mid`: with layer(t) = t // 16: every entry of box t lies in a layer 2 or 3 away from layer(t); entry 0 is exactly 3 layers away. `far_top`: with layer(t) = t // 4: every entry of box t lies in a layer 2 or 3 away from layer(t); entry 0 is exactly 3 layers away.
All inputs are finite; a program needn't handle non-finite values.
Results may differ from a plain program's by a relative error of at most 0.012.
Values may be sent and summed in bfloat16 or wider, within the bound.
A program may use at most 192 MiB of HBM per device.

v0:
```python
import jax
import jax.numpy as jnp
from jax import lax
from jax.sharding import PartitionSpec as P

SIDE = 8
relax_step = 0.1


def padded(cells, sides, width):
    for axis, dim in sides:
        count = lax.axis_size(axis)
        ends = count - 1
        head = lax.slice_in_dim(cells, 0, width, axis=dim)
        tail = lax.slice_in_dim(cells, cells.shape[dim] - width, cells.shape[dim], axis=dim)
        cells = jnp.concatenate(
            [
                lax.ppermute(tail, axis, [(i, (i + 1) % count) for i in range(ends)]),
                cells,
                lax.ppermute(head, axis, [((i + 1) % count, i) for i in range(ends)]),
            ],
            axis=dim,
        )
    return cells


def leaf_project(density, leaf_basis):
    return jnp.einsum(
        "olp,rp->lor", density, leaf_basis, preferred_element_type=jnp.float32
    ).astype(jnp.bfloat16)


def octant_up(moments, side_boxes, transfer):
    node_count, orbits, rank_width = moments.shape
    layers = node_count // (side_boxes * side_boxes)
    half_side = side_boxes // 2
    shaped = moments.reshape(layers // 2, 2, half_side, 2, half_side, 2, orbits, rank_width)
    octant_grid = transfer.reshape(2, 2, 2, rank_width, rank_width)
    parents = jnp.einsum(
        "apbqcuos,pqusr->abcor", shaped, octant_grid, preferred_element_type=jnp.float32
    )
    return parents.reshape(-1, orbits, rank_width).astype(jnp.bfloat16)


def octant_down(coeffs, side_boxes, transfer):
    node_count, orbits, rank_width = coeffs.shape
    layers = node_count // (side_boxes * side_boxes)
    shaped = coeffs.reshape(layers, side_boxes, side_boxes, orbits, rank_width)
    octant_grid = transfer.reshape(2, 2, 2, rank_width, rank_width)
    children = jnp.einsum(
        "abcor,pqusr->apbqcuos", shaped, octant_grid, preferred_element_type=jnp.float32
    )
    return children.reshape(-1, orbits, rank_width)


def couple_rows(moments, sources, coupling, scale):
    node_count, orbits, rank_width = moments.shape
    flattened = moments.reshape(node_count, orbits * rank_width)
    identity = jnp.eye(orbits, dtype=coupling.dtype)
    running = None
    for column_start in range(0, sources.shape[1], 27):
        block_coupling = coupling[column_start : column_start + 27]
        widened = jnp.einsum("ab,krs->kasbr", identity, block_coupling).reshape(
            block_coupling.shape[0], orbits * rank_width, orbits * rank_width
        )
        picked = jnp.take(flattened, sources[:, column_start : column_start + 27], axis=0)
        piece_sum = jnp.einsum("lkx,kxy->ly", picked, widened, preferred_element_type=jnp.float32)
        running = piece_sum if running is None else running + piece_sum
    return scale * running.reshape(-1, orbits, rank_width)


def near_sum(density, sources, near_table):
    running = None
    for column_start in range(0, sources.shape[1], 9):
        picked = jnp.take(density, sources[:, column_start : column_start + 9], axis=1)
        piece_sum = jnp.einsum(
            "olkq,kpq->olp",
            picked,
            near_table[column_start : column_start + 9],
            preferred_element_type=jnp.float32,
        )
        running = piece_sum if running is None else running + piece_sum
    return running


def shifted(values, offset):
    node_count = values.shape[0]
    if abs(offset) >= node_count:
        return jnp.zeros_like(values)
    empty = jnp.zeros((abs(offset), values.shape[1], values.shape[2]), values.dtype)
    if offset > 0:
        return jnp.concatenate([values[offset:], empty], axis=0)
    return jnp.concatenate([empty, values[:offset]], axis=0)


def coarse_couple(moments, coarse_coupling, scale):
    node_count = moments.shape[0]
    odd_rows = (jnp.arange(node_count) % 2).astype(jnp.float32)[:, None, None]
    even_rows = 1.0 - odd_rows

    def apply_matrix(which, offset):
        return jnp.einsum(
            "nos,rs->nor",
            shifted(moments, offset),
            coarse_coupling[which],
            preferred_element_type=jnp.float32,
        )

    running = (
        apply_matrix(1, -2)
        + apply_matrix(2, 2)
        + even_rows * apply_matrix(3, 3)
        + odd_rows * apply_matrix(0, -3)
    )
    return scale * running


def coarse_up(moments, pair_transfer):
    node_count, orbits, rank_width = moments.shape
    shaped = moments.reshape(-1, 2, orbits, rank_width)
    return jnp.einsum(
        "apos,psr->aor", shaped, pair_transfer, preferred_element_type=jnp.float32
    ).astype(jnp.bfloat16)


def coarse_down(coeffs, pair_transfer):
    children = jnp.einsum(
        "aor,psr->apos", coeffs, pair_transfer, preferred_element_type=jnp.float32
    )
    return children.reshape(-1, coeffs.shape[1], coeffs.shape[2])


def coarse_tree(cube_moments, coarse_coupling, pair_transfer):
    levels = [cube_moments]
    while levels[-1].shape[0] > 1:
        levels.append(coarse_up(levels[-1], pair_transfer))
    top_level = len(levels) - 1
    coeffs = coarse_couple(levels[top_level], coarse_coupling, 0.5 ** (3 + top_level)).astype(
        jnp.bfloat16
    )
    for depth_level in range(top_level - 1, -1, -1):
        pushed = coarse_down(coeffs, pair_transfer)
        coupled = coarse_couple(levels[depth_level], coarse_coupling, 0.5 ** (3 + depth_level))
        coeffs = (coupled + pushed).astype(jnp.bfloat16)
    return coeffs


def shards(
    orbitals,
    near_source,
    far_leaf,
    far_mid,
    far_top,
    leaf_basis,
    near_table,
    transfer,
    coupling,
    pair_transfer,
    coarse_coupling,
):
    orbits, leaf_count, points = orbitals.shape
    rank_size = leaf_basis.shape[0]
    device = lax.axis_index("space")
    density = (orbitals * orbitals).astype(jnp.bfloat16)
    layer_size = SIDE * SIDE
    reach_leaves = 12 * layer_size
    density_ext = padded(density, (("space", 1),), layer_size)
    near_start = device * leaf_count - layer_size
    local_moments = leaf_project(density, leaf_basis)
    flattened = local_moments.reshape(leaf_count, orbits * rank_size)
    leaf_ext = padded(flattened, (("space", 0),), reach_leaves).reshape(-1, orbits, rank_size)
    near_field = near_sum(density_ext, near_source - near_start, near_table)
    mid_ext = octant_up(leaf_ext, SIDE, transfer)
    top_ext = octant_up(mid_ext, SIDE // 2, transfer)
    top_count = leaf_count // 64
    mid_count = leaf_count // 8
    top_rim = reach_leaves // 64
    mid_rim = reach_leaves // 8
    top_local = top_ext[top_rim : top_rim + top_count]
    cube_local = octant_up(top_local, SIDE // 4, transfer)
    cube_rows = cube_local.shape[0]
    cube_all = lax.all_gather(
        cube_local.reshape(cube_rows, orbits * rank_size), "space", axis=0, tiled=True
    ).reshape(-1, orbits, rank_size)
    cube_coeffs = coarse_tree(cube_all, coarse_coupling, pair_transfer)
    cube_own = lax.dynamic_slice_in_dim(cube_coeffs, device * cube_rows, cube_rows, 0)
    top_coeffs = (
        couple_rows(top_ext, far_top - (device * top_count - top_rim), coupling, 0.25)
        + octant_down(cube_own, SIDE // 8, transfer)
    ).astype(jnp.bfloat16)
    mid_coeffs = (
        couple_rows(mid_ext, far_mid - (device * mid_count - mid_rim), coupling, 0.5)
        + octant_down(top_coeffs, SIDE // 4, transfer)
    ).astype(jnp.bfloat16)
    leaf_coeffs = (
        couple_rows(leaf_ext, far_leaf - (device * leaf_count - reach_leaves), coupling, 1.0)
        + octant_down(mid_coeffs, SIDE // 2, transfer)
    ).astype(jnp.bfloat16)
    far_field = jnp.einsum(
        "lor,rp->olp", leaf_coeffs, leaf_basis, preferred_element_type=jnp.float32
    )
    potential = near_field + far_field
    hartree = lax.psum(jnp.sum(potential, axis=0).astype(jnp.bfloat16), "orb").astype(jnp.float32)
    return orbitals - relax_step * (hartree[None] - potential) * orbitals


def solution(mesh):
    placed = (
        P("orb", "space", None),
        P("space", None),
        P("space", None),
        P("space", None),
        P("space", None),
        P(),
        P(),
        P(),
        P(),
        P(),
        P(),
    )
    return jax.shard_map(
        shards, mesh=mesh, in_specs=placed, out_specs=P("orb", "space", None), check_vma=False
    )
```

profile of v0, /device:TPU:0, one launch (start us, length us, event | category | flops | bytes accessed | tf_op | source)
XLA Modules:
  0.0 1078.0 jit_solution(17902328975907240493)
XLA Ops:
  15.3 4.8 collective-permute-start
  55.0 9.0 multiply_bitcast_fusion
  77.4 4.4 reshape.258
  105.5 7.3 copy.392
  112.7 71.8 %gather_fusion.2 = bf16[9216,2,256]{2,1,0:T(2,128)(2,1)} fusion(bf16[2,1152,256]{2,0,1:T(2,128)(2,1)S(1)} %copy.392, s32[9216]{0:T(1024)S(1)} %broadcast_clamp_fusion.4), kind=kCustom, calls=%fused_computation.5.clone | custom fusion | bytes 18911232 | tf_op jit(solution)/shard_map/jit(_take)/gather | solution.py:75
  184.6 71.8 %gather_fusion.1 = bf16[9216,2,256]{2,1,0:T(2,128)(2,1)} fusion(bf16[2,1152,256]{2,0,1:T(2,128)(2,1)S(1)} %copy.392, s32[9216]{0:T(1024)S(1)} %broadcast_clamp_fusion.5), kind=kCustom, calls=%fused_computation.4.clone | custom fusion | bytes 18911232 | tf_op jit(solution)/shard_map/jit(_take)/gather | solution.py:75
  256.4 71.8 %gather_fusion = bf16[9216,2,256]{2,1,0:T(2,128)(2,1)} fusion(bf16[2,1152,256]{2,0,1:T(2,128)(2,1)S(1)} %copy.392, s32[9216]{0:T(1024)S(1)} %broadcast_clamp_fusion.6), kind=kCustom, calls=%fused_computation.clone | custom fusion | bytes 18911232 | tf_op jit(solution)/shard_map/jit(_take)/gather | solution.py:75
  328.2 18.5 %fusion.2 = bf16[2,1024,9,256]{3,0,2,1:T(2,128)(2,1)S(1)} fusion(bf16[1024,9,2,256]{3,2,1,0:T(2,128)(2,1)} %bitcast.386, pred[1024,9]{1,0:T(8,128)(4,1)S(1)} %copy-done.18), kind=kLoop, calls=%fused_computation.20 | loop fusion | flops 4718592 | bytes 18883584 | tf_op jit(solution)/shard_map/jit(_take)/select_n | solution.py:75
  350.8 16.6 %fusion.1 = bf16[2,1024,9,256]{3,0,2,1:T(2,128)(2,1)S(1)} fusion(bf16[1024,9,2,256]{3,2,1,0:T(2,128)(2,1)S(1)} %bitcast.385, pred[1024,9]{1,0:T(8,128)(4,1)S(1)} %copy-done.19), kind=kLoop, calls=%fused_computation.19 | loop fusion | flops 4718592 | bytes 18883584 | tf_op jit(solution)/shard_map/jit(_take)/select_n | solution.py:75
  367.5 18.0 %fusion = bf16[2,1024,9,256]{3,0,2,1:T(2,128)(2,1)} fusion(bf16[1024,9,2,256]{3,2,1,0:T(2,128)(2,1)S(1)} %bitcast.382, pred[1024,9]{1,0:T(8,128)(4,1)S(1)} %copy-done.20), kind=kLoop, calls=%fused_computation.18 | loop fusion | flops 4718592 | bytes 18883584 | tf_op jit(solution)/shard_map/jit(_take)/select_n | solution.py:75
  395.6 28.1 %all-gather = bf16[32,2,128]{2,1,0:T(2,128)(2,1)S(1)} all-gather(bf16[1,2,128]{2,1,0:T(2,128)(2,1)S(1)} %reshape.425), channel_id=1, replica_groups=mesh['space'=32,'orb'=4] {'space'}, dimensions={0}, use_global_device_ids=true | all-gather | bytes 16896 | tf_op jit(solution)/shard_map/all_gather | solution.py:182
  449.5 8.2 gather_fusion.10
  463.2 7.1 gather_fusion.9
  475.8 7.1 gather_fusion.8
  488.4 7.1 gather_fusion.7
  504.7 96.4 %gather_fusion.3 = bf16[27648,128]{1,0:T(8,128)(2,1)} fusion(bf16[2560,128]{1,0:T(8,128)(2,1)S(1)} %pad_maximum_fusion.1, s32[27648]{0:T(1024)S(1)} %broadcast_clamp_fusion.3), kind=kCustom, calls=%fused_computation.1.clone | custom fusion | bytes 14266368 | tf_op jit(solution)/shard_map/jit(_take)/gather | solution.py:66
  601.1 11.9 %reshape.448 = bf16[1024,27,128]{2,1,0:T(8,128)(2,1)} reshape(bf16[27648,128]{1,0:T(8,128)(2,1)} %gather_fusion.3) | data formatting | bytes 14155776 | tf_op jit(solution)/shard_map/jit(_take)/gather | solution.py:66
  613.1 15.5 %broadcast_select_fusion.6 = bf16[1024,27,128]{2,1,0:T(8,128)(2,1)S(1)} fusion(bf16[1024,27,128]{2,1,0:T(8,128)(2,1)} %reshape.448, pred[1024,27]{1,0:T(8,128)(4,1)S(1)} %copy-done.17), kind=kLoop, calls=%fused_computation.30 | loop fusion | flops 3538944 | bytes 14183424 | tf_op jit(solution)/shard_map/jit(_take)/select_n | solution.py:66
  632.9 96.4 %gather_fusion.4 = bf16[27648,128]{1,0:T(8,128)(2,1)} fusion(bf16[2560,128]{1,0:T(8,128)(2,1)S(1)} %pad_maximum_fusion.1, s32[27648]{0:T(1024)S(1)} %broadcast_clamp_fusion.2), kind=kCustom, calls=%fused_computation.6.clone | custom fusion | bytes 14266368 | tf_op jit(solution)/shard_map/jit(_take)/gather | solution.py:66
  729.3 11.9 %reshape.452 = bf16[1024,27,128]{2,1,0:T(8,128)(2,1)} reshape(bf16[27648,128]{1,0:T(8,128)(2,1)} %gather_fusion.4) | data formatting | bytes 14155776 | tf_op jit(solution)/shard_map/jit(_take)/gather | solution.py:66
  741.2 96.4 %gather_fusion.5 = bf16[27648,128]{1,0:T(8,128)(2,1)} fusion(bf16[2560,128]{1,0:T(8,128)(2,1)S(1)} %pad_maximum_fusion.1, s32[27648]{0:T(1024)S(1)} %broadcast_clamp_fusion.1), kind=kCustom, calls=%fused_computation.7.clone | custom fusion | bytes 14266368 | tf_op jit(solution)/shard_map/jit(_take)/gather | solution.py:66
  837.6 11.9 %reshape.456 = bf16[1024,27,128]{2,1,0:T(8,128)(2,1)} reshape(bf16[27648,128]{1,0:T(8,128)(2,1)} %gather_fusion.5) | data formatting | bytes 14155776 | tf_op jit(solution)/shard_map/jit(_take)/gather | solution.py:66
  849.5 96.4 %gather_fusion.6 = bf16[27648,128]{1,0:T(8,128)(2,1)} fusion(bf16[2560,128]{1,0:T(8,128)(2,1)S(1)} %pad_maximum_fusion.1, s32[27648]{0:T(1024)S(1)} %copy-done.4), kind=kCustom, calls=%fused_computation.8.clone | custom fusion | bytes 14266368 | tf_op jit(solution)/shard_map/jit(_take)/gather | solution.py:66
  945.9 11.9 %reshape.460 = bf16[1024,27,128]{2,1,0:T(8,128)(2,1)} reshape(bf16[27648,128]{1,0:T(8,128)(2,1)} %gather_fusion.6) | data formatting | bytes 14155776 | tf_op jit(solution)/shard_map/jit(_take)/gather | solution.py:66
  957.9 15.4 %broadcast_select_fusion.5 = bf16[1024,27,128]{2,1,0:T(8,128)(2,1)S(1)} fusion(bf16[1024,27,128]{2,1,0:T(8,128)(2,1)} %reshape.452, pred[1024,27]{1,0:T(8,128)(4,1)S(1)} %copy-done.14), kind=kLoop, calls=%fused_computation.29 | loop fusion | flops 3538944 | bytes 14183424 | tf_op jit(solution)/shard_map/jit(_take)/select_n | solution.py:66
  973.3 4.3 fusion.37
  977.7 15.7 %broadcast_select_fusion.4 = bf16[1024,27,128]{2,1,0:T(8,128)(2,1)S(1)} fusion(bf16[1024,27,128]{2,1,0:T(8,128)(2,1)} %reshape.456, pred[1024,27]{1,0:T(8,128)(4,1)S(1)} %copy-done.15), kind=kLoop, calls=%fused_computation.28 | loop fusion | flops 3538944 | bytes 14183424 | tf_op jit(solution)/shard_map/jit(_take)/select_n | solution.py:66
  993.5 4.3 fusion.34
  997.8 13.7 %broadcast_select_fusion.3 = bf16[1024,27,128]{2,1,0:T(8,128)(2,1)S(1)} fusion(bf16[1024,27,128]{2,1,0:T(8,128)(2,1)S(1)} %bitcast.388, pred[1024,27]{1,0:T(8,128)(4,1)S(1)} %copy-done.16), kind=kLoop, calls=%fused_computation.27 | loop fusion | flops 3538944 | bytes 14183424 | tf_op jit(solution)/shard_map/jit(_take)/select_n | solution.py:66
  1011.6 4.3 fusion.31
  1016.5 7.0 fusion.300
  1023.5 43.0 %all-reduce.22.cloned.1.call-done = bf16[1024,256]{1,0:T(8,128)(2,1)} async-done(((bf16[1024,256]{1,0:T(8,128)(2,1)}), bf16[1024,256]{1,0:T(8,128)(2,1)}) %all-reduce.22.cloned.1.call-update) | async-done | bytes 524304 | tf_op jit(solution)/shard_map/psum | solution.py:203
  (335 shorter events, 154.4 us)
Async XLA Ops:
  6.5 387.6 %copy-start = (bf16[8,64,64]{2,1,0:T(8,128)(2,1)S(1)}, bf16[8,64,64]{2,1,0:T(8,128)(2,1)}, u32[]{:S(2)}) copy-start(bf16[8,64,64]{2,1,0:T(8,128)(2,1)} %param.26) | copy-start | bytes 196612
  6.5 29.9 %copy-start.11 = (bf16[4,64,64]{2,1,0:T(8,128)(2,1)S(1)}, bf16[4,64,64]{2,1,0:T(8,128)(2,1)}, u32[]{:S(2)}) copy-start(bf16[4,64,64]{2,1,0:T(8,128)(2,1)} %param.29) | copy-start | bytes 98308
  6.5 25.2 %copy-start.24 = (s32[1024,108]{0,1:T(8,128)S(1)}, s32[1024,108]{0,1:T(8,128)}, u32[]{:S(2)}) copy-start(s32[1024,108]{0,1:T(8,128)} %param.21) | copy-start | bytes 1327108
  6.5 30.7 %copy-start.9 = (bf16[2,64,64]{2,1,0:T(8,128)(2,1)S(1)}, bf16[2,64,64]{2,1,0:T(8,128)(2,1)}, u32[]{:S(2)}) copy-start(bf16[2,64,64]{2,1,0:T(8,128)(2,1)} %param.28) | copy-start | bytes 49156
  6.5 34.3 %copy-start.2 = (bf16[108,64,64]{0,2,1:T(8,128)(2,1)S(1)}, bf16[108,64,64]{0,2,1:T(8,128)(2,1)}, u32[]{:S(2)}) copy-start(bf16[108,64,64]{0,2,1:T(8,128)(2,1)} %param.27) | copy-start | bytes 2654212
  6.5 1059.9 %all-reduce.22.cloned.1.call-start = ((), (), s32[]{:S(2)}) async-start(), calls=%async_computation | async-start | bytes 1048576 | tf_op jit(solution)/shard_map/psum | solution.py:203
  10.5 379.0 %collective-permute-start.2 = (bf16[768,128]{1,0:T(8,128)(2,1)}, bf16[768,128]{1,0:T(8,128)(2,1)}, u32[]{:S(2)}, u32[]{:S(2)}) collective-permute-start(bf16[768,128]{1,0:T(8,128)(2,1)} %copy.403), channel_id=1, source_target_pairs={{0,4},{4,8},{8,12},{12,16},{16,20},{20,24},{24,28},{28,32},{32,36}... | collective-permute-start | bytes 589832 | tf_op jit(solution)/shard_map/ppermute | solution.py:18
  13.3 376.3 %collective-permute-start.3 = (bf16[768,128]{1,0:T(8,128)(2,1)}, bf16[768,128]{1,0:T(8,128)(2,1)}, u32[]{:S(2)}, u32[]{:S(2)}) collective-permute-start(bf16[768,128]{1,0:T(8,128)(2,1)} %copy.404), channel_id=1, source_target_pairs={{4,0},{8,4},{12,8},{16,12},{20,16},{24,20},{28,24},{32,28},{36,32}... | collective-permute-start | bytes 589832 | tf_op jit(solution)/shard_map/ppermute | solution.py:20
  15.3 89.3 %collective-permute-start = (bf16[2,64,256]{2,1,0:T(8,128)(2,1)}, bf16[2,64,256]{2,1,0:T(8,128)(2,1)}, u32[]{:S(2)}, u32[]{:S(2)}) collective-permute-start(bf16[2,64,256]{2,1,0:T(8,128)(2,1)} %get-tuple-element.6), channel_id=1, source_target_pairs={{0,4},{4,8},{8,12},{12,16},{16,20},{20,24},{24,28},{28,32},{32,36}... | collective-permute-start | bytes 196616 | tf_op jit(solution)/shard_map/ppermute | solution.py:18
  20.1 84.4 %collective-permute-start.1 = (bf16[2,64,256]{2,1,0:T(8,128)(2,1)}, bf16[2,64,256]{2,1,0:T(8,128)(2,1)}, u32[]{:S(2)}, u32[]{:S(2)}) collective-permute-start(bf16[2,64,256]{2,1,0:T(8,128)(2,1)} %get-tuple-element.8), channel_id=1, source_target_pairs={{4,0},{8,4},{12,8},{16,12},{20,16},{24,20},{28,24},{32,28},{36,32}... | collective-permute-start | bytes 196616 | tf_op jit(solution)/shard_map/ppermute | solution.py:20
  64.0 19.5 %copy-start.35 = (s32[128,27]{0,1:T(8,128)S(1)}, s32[128,27]{0,1:T(8,128)}, u32[]{:S(2)}) copy-start(s32[128,27]{0,1:T(8,128)} %get-tuple-element.37) | copy-start | bytes 41476
  64.0 20.4 %copy-start.41 = (pred[128,27]{0,1:T(8,128)(4,1)S(1)}, pred[128,27]{0,1:T(8,128)(4,1)}, u32[]{:S(2)}) copy-start(pred[128,27]{0,1:T(8,128)(4,1)} %get-tuple-element.33) | copy-start | bytes 10372
  64.0 25.9 %copy-start.23 = (s32[1024,27]{0,1:T(8,128)S(1)}, s32[1024,27]{0,1:T(8,128)}, u32[]{:S(2)}) copy-start(s32[1024,27]{0,1:T(8,128)} %get-tuple-element.21) | copy-start | bytes 331780
  64.0 27.3 %copy-start.22 = (s32[1024,27]{0,1:T(8,128)S(1)}, s32[1024,27]{0,1:T(8,128)}, u32[]{:S(2)}) copy-start(s32[1024,27]{0,1:T(8,128)} %get-tuple-element.20) | copy-start | bytes 331780
  67.5 26.1 %copy-start.21 = (s32[1024,27]{0,1:T(8,128)S(1)}, s32[1024,27]{0,1:T(8,128)}, u32[]{:S(2)}) copy-start(s32[1024,27]{0,1:T(8,128)} %get-tuple-element.19) | copy-start | bytes 331780
  73.2 26.3 %copy-start.29 = (s32[1024,9]{0,1:T(8,128)S(1)}, s32[1024,9]{0,1:T(8,128)}, u32[]{:S(2)}) copy-start(s32[1024,9]{0,1:T(8,128)} %get-tuple-element.30) | copy-start | bytes 110596
  77.4 24.3 %copy-start.28 = (s32[1024,9]{0,1:T(8,128)S(1)}, s32[1024,9]{0,1:T(8,128)}, u32[]{:S(2)}) copy-start(s32[1024,9]{0,1:T(8,128)} %get-tuple-element.28) | copy-start | bytes 110596
  256.4 71.8 %copy-start.18 = (pred[1024,9]{1,0:T(8,128)(4,1)S(1)}, pred[1024,9]{1,0:T(8,128)(4,1)}, u32[]{:S(2)}) copy-start(pred[1024,9]{1,0:T(8,128)(4,1)} %copy.398) | copy-start | bytes 27652
  328.2 22.5 %slice-start.3 = ((s8[9437184]{0:T(1024)(128)(4,1)}), s8[4194304]{0:T(1024)(128)(4,1)S(1)}, s32[]{:S(2)}) async-start(s8[9437184]{0:T(1024)(128)(4,1)} %bitcast.383), calls=%async_computation.4 | async-start | bytes 8388608
  328.2 22.5 %slice-start.4 = ((s8[9437184]{0:T(1024)(128)(4,1)}), s8[4194304]{0:T(1024)(128)(4,1)S(1)}, s32[]{:S(2)}) async-start(s8[9437184]{0:T(1024)(128)(4,1)} %bitcast.383), calls=%async_computation.5 | async-start | bytes 8388608
  346.7 20.7 %slice-start = ((s8[9437184]{0:T(1024)(128)(4,1)}), s8[4194304]{0:T(1024)(128)(4,1)S(1)}, s32[]{:S(2)}) async-start(s8[9437184]{0:T(1024)(128)(4,1)} %bitcast.380), calls=%async_computation.1 | async-start | bytes 8388608
  346.7 20.7 %slice-start.1 = ((s8[9437184]{0:T(1024)(128)(4,1)}), s8[1048576]{0:T(1024)(128)(4,1)S(1)}, s32[]{:S(2)}) async-start(s8[9437184]{0:T(1024)(128)(4,1)} %bitcast.380), calls=%async_computation.2 | async-start | bytes 2097152
  389.5 34.2 %copy-start.10 = (bf16[2,64,64]{2,1,0:T(8,128)(2,1)S(1)}, bf16[2,64,64]{2,1,0:T(8,128)(2,1)}, u32[]{:S(2)}) copy-start(bf16[2,64,64]{2,1,0:T(8,128)(2,1)} %param.28) | copy-start | bytes 49156
  389.5 35.2 %copy-start.12 = (bf16[4,64,64]{2,1,0:T(8,128)(2,1)S(1)}, bf16[4,64,64]{2,1,0:T(8,128)(2,1)}, u32[]{:S(2)}) copy-start(bf16[4,64,64]{2,1,0:T(8,128)(2,1)} %param.29) | copy-start | bytes 98308
  389.5 47.4 %copy-start.37 = (s32[1024]{0:T(1024)S(1)}, s32[1024]{0:T(1024)}, u32[]{:S(2)}) copy-start(s32[1024]{0:T(1024)} %pad_clamp_fusion.7) | copy-start | bytes 12292
  389.5 49.0 %copy-start.38 = (s32[1024]{0:T(1024)S(1)}, s32[1024]{0:T(1024)}, u32[]{:S(2)}) copy-start(s32[1024]{0:T(1024)} %pad_clamp_fusion.6) | copy-start | bytes 12292
  389.6 51.2 %copy-start.39 = (s32[1024]{0:T(1024)S(1)}, s32[1024]{0:T(1024)}, u32[]{:S(2)}) copy-start(s32[1024]{0:T(1024)} %pad_clamp_fusion.5) | copy-start | bytes 12292
  394.7 54.3 %copy-start.6 = (bf16[27,128,128]{2,1,0:T(8,128)(2,1)S(1)}, bf16[27,128,128]{2,1,0:T(8,128)(2,1)}, u32[]{:S(2)}) copy-start(bf16[27,128,128]{2,1,0:T(8,128)(2,1)} %reshape.258) | copy-start | bytes 2654212
  973.3 24.5 %slice-start.6 = ((s8[8388608]{0:T(1024)(128)(4,1)}), s8[4194304]{0:T(1024)(128)(4,1)S(1)}, s32[]{:S(2)}) async-start(s8[8388608]{0:T(1024)(128)(4,1)} %bitcast.387), calls=%async_computation.7 | async-start | bytes 8388608
  977.7 20.1 %slice-start.7 = ((s8[8388608]{0:T(1024)(128)(4,1)}), s8[4194304]{0:T(1024)(128)(4,1)S(1)}, s32[]{:S(2)}) async-start(s8[8388608]{0:T(1024)(128)(4,1)} %bitcast.387), calls=%async_computation.8 | async-start | bytes 8388608
  1016.5 51.1 %copy-start.3 = (f32[2,1024,256]{2,1,0:T(8,128)S(1)}, f32[2,1024,256]{2,1,0:T(8,128)}, u32[]{:S(2)}) copy-start(f32[2,1024,256]{2,1,0:T(8,128)} %param.19) | copy-start | bytes 6291460
  1016.5 54.3 %copy-start.1 = (bf16[8,64,64]{2,1,0:T(8,128)(2,1)S(1)}, bf16[8,64,64]{2,1,0:T(8,128)(2,1)}, u32[]{:S(2)}) copy-start(bf16[8,64,64]{2,1,0:T(8,128)(2,1)} %param.26) | copy-start | bytes 196612
  (31 other events, 372.2 us)
Sparse Core Ops, SparseCore 0:
  1023.6 42.8 all-reduce.21
where the time goes:
time: 1090 us; the launch traced here: 1080 us
  local copies, waits for them, and re-layouts  761 us (70%)
  other arithmetic  162 us (15%)
  matrix products  58.8 us (5%)
  waiting for transfers between devices  43 us (4%)
  blocking collectives  28.1 us (3%)
  between operations  15 us (1%)
    gather x24, local copies, waits for them, and re-layouts, couple_rows(): jnp.take(flattened, sources[:, column_start:column_start + 27], axis=0)  475 us
    gather x3, local copies, waits for them, and re-layouts, near_sum(): jnp.take(density, sources[:, column_start:column_start + 9], axis=1)  215 us
    select_n x13, other arithmetic, couple_rows(): jnp.take(flattened, sources[:, column_start:column_start + 27], axis=0)  74.5 us
    select_n x4, other arithmetic, near_sum(): jnp.take(density, sources[:, column_start:column_start + 9], axis=1)  53.8 us
    psum x1, waiting for transfers between devices, shards(): lax.psum(jnp.sum(potential, axis=0).astype(jnp.bfloat16), 'orb')  43 us
    all_gather x1, blocking collectives, shards(): lax.all_gather(cube_local.reshape(cube_rows, orbits * rank_size), 'space'...  28.1 us
    dot_general x12, matrix products, couple_rows(): jnp.einsum('lkx,kxy->ly', picked, widened, preferred_element_type=jnp.flo...  26 us
  transfers between devices with their start and end apart: 5, of which 1 were waited for; matrix products, arithmetic and copies ran while one was open for 34% of the time, Pallas kernels for 0%

commit v1 on v0

--- a/solution.py
+++ b/solution.py
@@ -5,6 +5,13 @@
 
 SIDE = 8
 relax_step = 0.1
+
+
+def exchange_gather(value, axis, along):
+    n_dev = lax.axis_size(axis)
+    blocks = jnp.stack([value for _ in range(n_dev)])
+    blocks = lax.all_to_all(blocks, axis, split_axis=0, concat_axis=0)
+    return jnp.concatenate(blocks, axis=along)
 
 
 def padded(cells, sides, width):
@@ -179,8 +186,8 @@
     top_local = top_ext[top_rim : top_rim + top_count]
     cube_local = octant_up(top_local, SIDE // 4, transfer)
     cube_rows = cube_local.shape[0]
-    cube_all = lax.all_gather(
-        cube_local.reshape(cube_rows, orbits * rank_size), "space", axis=0, tiled=True
+    cube_all = exchange_gather(
+        cube_local.reshape(cube_rows, orbits * rank_size), "space", 0
     ).reshape(-1, orbits, rank_size)
     cube_coeffs = coarse_tree(cube_all, coarse_coupling, pair_transfer)
     cube_own = lax.dynamic_slice_in_dim(cube_coeffs, device * cube_rows, cube_rows, 0)

time: 1090 us -> 1050 us (0.963)
  blocking collectives: 28.1 us -> 0 us
  other arithmetic: 162 us -> 150 us
  starting transfers between devices: 9.42 us -> 21.3 us
    all_gather x1 -> x0, blocking collectives: 28.1 us -> none  [shards(): lax.all_gather(cube_local.reshape(cube_rows, orbits * rank_size), 'space'...]
    all_to_all x0 -> x1, starting transfers between devices: none -> 11.9 us  [exchange_gather(): blocks = lax.all_to_all(blocks, axis, split_axis=0, concat_axis=0)]
    select_n x13, other arithmetic: 74.5 us -> 63.2 us  [couple_rows(): jnp.take(flattened, sources[:, column_start:column_start + 27], axis=0)]
  transfers between devices with their start and end apart: 5 -> 6, of which waited for: 1 -> 1; matrix products, arithmetic and copies ran while one was open for 34% -> 89% of each run, Pallas kernels for 0% -> 0%
where the time goes in v1:
time: 1050 us
  local copies, waits for them, and re-layouts  760 us (72%)
  other arithmetic  150 us (14%)
  matrix products  54.6 us (5%)
  waiting for transfers between devices  44.4 us (4%)
  starting transfers between devices  21.3 us (2%)
  between operations  15.3 us (1%)
    gather x24, local copies, waits for them, and re-layouts, couple_rows(): jnp.take(flattened, sources[:, column_start:column_start + 27], axis=0)  475 us
    gather x3, local copies, waits for them, and re-layouts, near_sum(): jnp.take(density, sources[:, column_start:column_start + 9], axis=1)  215 us
    select_n x13, other arithmetic, couple_rows(): jnp.take(flattened, sources[:, column_start:column_start + 27], axis=0)  63.2 us
    select_n x4, other arithmetic, near_sum(): jnp.take(density, sources[:, column_start:column_start + 9], axis=1)  53.4 us
    psum x1, waiting for transfers between devices, shards(): lax.psum(jnp.sum(potential, axis=0).astype(jnp.bfloat16), 'orb')  44.4 us
    dot_general x12, matrix products, couple_rows(): jnp.einsum('lkx,kxy->ly', picked, widened, preferred_element_type=jnp.flo...  25.9 us
  transfers between devices with their start and end apart: 6, of which 1 were waited for; matrix products, arithmetic and copies ran while one was open for 89% of the time, Pallas kernels for 0%

profile of v1, /device:TPU:0, one launch (start us, length us, event | category | flops | bytes accessed | tf_op | source)
XLA Modules:
  0.0 1045.7 jit_solution(13487662152618142036)
XLA Ops:
  15.2 4.9 collective-permute-start
  54.8 9.0 multiply_bitcast_fusion
  77.2 4.4 reshape.256
  103.7 7.3 copy.305
  111.0 71.8 %gather_fusion.2 = bf16[9216,2,256]{2,1,0:T(2,128)(2,1)} fusion(bf16[2,1152,256]{2,0,1:T(2,128)(2,1)S(1)} %copy.305, s32[9216]{0:T(1024)S(1)} %broadcast_clamp_fusion.4), kind=kCustom, calls=%fused_computation.5.clone | custom fusion | bytes 18911232 | tf_op jit(solution)/shard_map/jit(_take)/gather | solution.py:82
  182.8 71.9 %gather_fusion.1 = bf16[9216,2,256]{2,1,0:T(2,128)(2,1)} fusion(bf16[2,1152,256]{2,0,1:T(2,128)(2,1)S(1)} %copy.305, s32[9216]{0:T(1024)S(1)} %broadcast_clamp_fusion.5), kind=kCustom, calls=%fused_computation.4.clone | custom fusion | bytes 18911232 | tf_op jit(solution)/shard_map/jit(_take)/gather | solution.py:82
  254.6 71.8 %gather_fusion = bf16[9216,2,256]{2,1,0:T(2,128)(2,1)} fusion(bf16[2,1152,256]{2,0,1:T(2,128)(2,1)S(1)} %copy.305, s32[9216]{0:T(1024)S(1)} %broadcast_clamp_fusion.6), kind=kCustom, calls=%fused_computation.clone | custom fusion | bytes 18911232 | tf_op jit(solution)/shard_map/jit(_take)/gather | solution.py:82
  326.5 18.5 %fusion.2 = bf16[2,1024,9,256]{3,0,2,1:T(2,128)(2,1)S(1)} fusion(bf16[1024,9,2,256]{3,2,1,0:T(2,128)(2,1)} %bitcast.385, pred[1024,9]{1,0:T(8,128)(4,1)S(1)} %copy-done.22), kind=kLoop, calls=%fused_computation.20 | loop fusion | flops 4718592 | bytes 18883584 | tf_op jit(solution)/shard_map/jit(_take)/select_n | solution.py:82
  349.0 16.6 %fusion.1 = bf16[2,1024,9,256]{3,0,2,1:T(2,128)(2,1)S(1)} fusion(bf16[1024,9,2,256]{3,2,1,0:T(2,128)(2,1)S(1)} %bitcast.384, pred[1024,9]{1,0:T(8,128)(4,1)S(1)} %copy-done.23), kind=kLoop, calls=%fused_computation.19 | loop fusion | flops 4718592 | bytes 18883584 | tf_op jit(solution)/shard_map/jit(_take)/select_n | solution.py:82
  365.7 17.7 %fusion = bf16[2,1024,9,256]{3,0,2,1:T(2,128)(2,1)} fusion(bf16[1024,9,2,256]{3,2,1,0:T(2,128)(2,1)S(1)} %bitcast.381, pred[1024,9]{1,0:T(8,128)(4,1)S(1)} %copy-done.24), kind=kLoop, calls=%fused_computation.18 | loop fusion | flops 4718592 | bytes 18883584 | tf_op jit(solution)/shard_map/jit(_take)/select_n | solution.py:82
  394.0 11.9 %all-to-all-start = ((bf16[32,2,128]{2,1,0:T(2,128)(2,1)}), bf16[32,2,128]{2,1,0:T(2,128)(2,1)}, u32[]{:S(2)}, u32[]{:S(2)}) async-start(bf16[32,2,128]{2,1,0:T(2,128)(2,1)} %stack.3), calls=%async_computation | async-start | bytes 32768 | tf_op jit(solution)/shard_map/all_to_all | solution.py:13
  414.3 7.1 gather_fusion.10
  422.7 7.1 gather_fusion.9
  431.1 7.1 gather_fusion.8
  439.6 7.1 gather_fusion.7
  448.0 96.4 %gather_fusion.3 = bf16[27648,128]{1,0:T(8,128)(2,1)} fusion(bf16[2560,128]{1,0:T(8,128)(2,1)S(1)} %pad_maximum_fusion.1, s32[27648]{0:T(1024)S(1)} %broadcast_clamp_fusion.3), kind=kCustom, calls=%fused_computation.1.clone | custom fusion | bytes 14266368 | tf_op jit(solution)/shard_map/jit(_take)/gather | solution.py:73
  544.4 11.9 %reshape.438 = bf16[1024,27,128]{2,1,0:T(8,128)(2,1)} reshape(bf16[27648,128]{1,0:T(8,128)(2,1)} %gather_fusion.3) | data formatting | bytes 14155776 | tf_op jit(solution)/shard_map/jit(_take)/gather | solution.py:73
  557.4 15.4 %broadcast_select_fusion.6 = bf16[1024,27,128]{2,1,0:T(8,128)(2,1)S(1)} fusion(bf16[1024,27,128]{2,1,0:T(8,128)(2,1)} %reshape.438, pred[1024,27]{1,0:T(8,128)(4,1)S(1)} %copy-done.21), kind=kLoop, calls=%fused_computation.30 | loop fusion | flops 3538944 | bytes 14183424 | tf_op jit(solution)/shard_map/jit(_take)/select_n | solution.py:73
  572.8 5.1 fusion.19
  577.9 96.4 %gather_fusion.4 = bf16[27648,128]{1,0:T(8,128)(2,1)} fusion(bf16[2560,128]{1,0:T(8,128)(2,1)S(1)} %pad_maximum_fusion.1, s32[27648]{0:T(1024)S(1)} %broadcast_clamp_fusion.2), kind=kCustom, calls=%fused_computation.6.clone | custom fusion | bytes 14266368 | tf_op jit(solution)/shard_map/jit(_take)/gather | solution.py:73
  674.3 11.9 %reshape.442 = bf16[1024,27,128]{2,1,0:T(8,128)(2,1)} reshape(bf16[27648,128]{1,0:T(8,128)(2,1)} %gather_fusion.4) | data formatting | bytes 14155776 | tf_op jit(solution)/shard_map/jit(_take)/gather | solution.py:73
  686.2 96.4 %gather_fusion.5 = bf16[27648,128]{1,0:T(8,128)(2,1)} fusion(bf16[2560,128]{1,0:T(8,128)(2,1)S(1)} %pad_maximum_fusion.1, s32[27648]{0:T(1024)S(1)} %broadcast_clamp_fusion.1), kind=kCustom, calls=%fused_computation.7.clone | custom fusion | bytes 14266368 | tf_op jit(solution)/shard_map/jit(_take)/gather | solution.py:73
  782.6 11.9 %reshape.446 = bf16[1024,27,128]{2,1,0:T(8,128)(2,1)} reshape(bf16[27648,128]{1,0:T(8,128)(2,1)} %gather_fusion.5) | data formatting | bytes 14155776 | tf_op jit(solution)/shard_map/jit(_take)/gather | solution.py:73
  794.6 96.4 %gather_fusion.6 = bf16[27648,128]{1,0:T(8,128)(2,1)} fusion(bf16[2560,128]{1,0:T(8,128)(2,1)S(1)} %pad_maximum_fusion.1, s32[27648]{0:T(1024)S(1)} %copy-done.7), kind=kCustom, calls=%fused_computation.8.clone | custom fusion | bytes 14266368 | tf_op jit(solution)/shard_map/jit(_take)/gather | solution.py:73
  891.0 12.2 %reshape.450 = bf16[1024,27,128]{2,1,0:T(8,128)(2,1)} reshape(bf16[27648,128]{1,0:T(8,128)(2,1)} %gather_fusion.6) | data formatting | bytes 14155776 | tf_op jit(solution)/shard_map/jit(_take)/gather | solution.py:73
  913.2 13.7 %broadcast_select_fusion.5 = bf16[1024,27,128]{2,1,0:T(8,128)(2,1)S(1)} fusion(bf16[1024,27,128]{2,1,0:T(8,128)(2,1)S(1)} %bitcast.391, pred[1024,27]{1,0:T(8,128)(4,1)S(1)} %copy-done.18), kind=kLoop, calls=%fused_computation.29 | loop fusion | flops 3538944 | bytes 14183424 | tf_op jit(solution)/shard_map/jit(_take)/select_n | solution.py:73
  927.0 4.3 fusion.37
  931.4 13.7 %broadcast_select_fusion.4 = bf16[1024,27,128]{2,1,0:T(8,128)(2,1)S(1)} fusion(bf16[1024,27,128]{2,1,0:T(8,128)(2,1)S(1)} %bitcast.389, pred[1024,27]{1,0:T(8,128)(4,1)S(1)} %copy-done.19), kind=kLoop, calls=%fused_computation.28 | loop fusion | flops 3538944 | bytes 14183424 | tf_op jit(solution)/shard_map/jit(_take)/select_n | solution.py:73
  945.2 5.1 fusion.34
  950.3 14.0 %broadcast_select_fusion.3 = bf16[1024,27,128]{2,1,0:T(8,128)(2,1)S(1)} fusion(bf16[1024,27,128]{2,1,0:T(8,128)(2,1)S(1)} %bitcast.387, pred[1024,27]{1,0:T(8,128)(4,1)S(1)} %copy-done.20), kind=kLoop, calls=%fused_computation.27 | loop fusion | flops 3538944 | bytes 14183424 | tf_op jit(solution)/shard_map/jit(_take)/select_n | solution.py:73
  979.1 10.7 %fusion.300 = (bf16[1024,256]{1,0:T(8,128)(2,1)}, f32[2,1024,256]{2,1,0:T(8,128)}) fusion(f32[1024,2,256]{2,0,1:T(8,128)S(1)} %fusion.103, f32[2,1024,256,1]{2,1,3,0:T(8,128)} %fusion.3, f32[2,1024,256,1]{2,1,3,0:T(8,128)} %fusion.5, bf16[27,256,256]{2,1,0:T(8,128)(2,1)} %param.25, bf16[2,1024,9,256]{3,0,2,1:T(2,128)(2,1)} %fusion), kind=kOutput, calls=%fused_computation.419 | convolution fusion | flops 2417754112 | bytes 19529728 | tf_op jit(solution)/shard_map/olkq,kpq->olp/dot_general | solution.py:83
  989.8 44.4 %all-reduce.22.cloned.1.call-done = bf16[1024,256]{1,0:T(8,128)(2,1)} async-done(((bf16[1024,256]{1,0:T(8,128)(2,1)}), bf16[1024,256]{1,0:T(8,128)(2,1)}) %all-reduce.22.cloned.1.call-update) | async-done | bytes 524304 | tf_op jit(solution)/shard_map/psum | solution.py:210
  (395 shorter events, 136.1 us)
Async XLA Ops:
  6.5 385.5 %copy-start = (bf16[8,64,64]{2,1,0:T(8,128)(2,1)S(1)}, bf16[8,64,64]{2,1,0:T(8,128)(2,1)}, u32[]{:S(2)}) copy-start(bf16[8,64,64]{2,1,0:T(8,128)(2,1)} %param.26) | copy-start | bytes 196612
  6.5 29.7 %copy-start.15 = (bf16[4,64,64]{2,1,0:T(8,128)(2,1)S(1)}, bf16[4,64,64]{2,1,0:T(8,128)(2,1)}, u32[]{:S(2)}) copy-start(bf16[4,64,64]{2,1,0:T(8,128)(2,1)} %param.29) | copy-start | bytes 98308
  6.5 24.9 %copy-start.29 = (s32[1024,108]{0,1:T(8,128)S(1)}, s32[1024,108]{0,1:T(8,128)}, u32[]{:S(2)}) copy-start(s32[1024,108]{0,1:T(8,128)} %param.21) | copy-start | bytes 1327108
  6.5 30.5 %copy-start.13 = (bf16[2,64,64]{2,1,0:T(8,128)(2,1)S(1)}, bf16[2,64,64]{2,1,0:T(8,128)(2,1)}, u32[]{:S(2)}) copy-start(bf16[2,64,64]{2,1,0:T(8,128)(2,1)} %param.28) | copy-start | bytes 49156
  6.5 34.1 %copy-start.1 = (bf16[108,64,64]{0,2,1:T(8,128)(2,1)S(1)}, bf16[108,64,64]{0,2,1:T(8,128)(2,1)}, u32[]{:S(2)}) copy-start(bf16[108,64,64]{0,2,1:T(8,128)(2,1)} %param.27) | copy-start | bytes 2654212
  10.5 376.9 %collective-permute-start.2 = (bf16[768,128]{1,0:T(8,128)(2,1)}, bf16[768,128]{1,0:T(8,128)(2,1)}, u32[]{:S(2)}, u32[]{:S(2)}) collective-permute-start(bf16[768,128]{1,0:T(8,128)(2,1)} %copy.316), channel_id=1, source_target_pairs={{0,4},{4,8},{8,12},{12,16},{16,20},{20,24},{24,28},{28,32},{32,36}... | collective-permute-start | bytes 589832 | tf_op jit(solution)/shard_map/ppermute | solution.py:25
  13.2 374.1 %collective-permute-start.3 = (bf16[768,128]{1,0:T(8,128)(2,1)}, bf16[768,128]{1,0:T(8,128)(2,1)}, u32[]{:S(2)}, u32[]{:S(2)}) collective-permute-start(bf16[768,128]{1,0:T(8,128)(2,1)} %copy.317), channel_id=1, source_target_pairs={{4,0},{8,4},{12,8},{16,12},{20,16},{24,20},{28,24},{32,28},{36,32}... | collective-permute-start | bytes 589832 | tf_op jit(solution)/shard_map/ppermute | solution.py:27
  15.2 87.5 %collective-permute-start = (bf16[2,64,256]{2,1,0:T(8,128)(2,1)}, bf16[2,64,256]{2,1,0:T(8,128)(2,1)}, u32[]{:S(2)}, u32[]{:S(2)}) collective-permute-start(bf16[2,64,256]{2,1,0:T(8,128)(2,1)} %get-tuple-element.6), channel_id=1, source_target_pairs={{0,4},{4,8},{8,12},{12,16},{16,20},{20,24},{24,28},{28,32},{32,36}... | collective-permute-start | bytes 196616 | tf_op jit(solution)/shard_map/ppermute | solution.py:25
  20.1 82.7 %collective-permute-start.1 = (bf16[2,64,256]{2,1,0:T(8,128)(2,1)}, bf16[2,64,256]{2,1,0:T(8,128)(2,1)}, u32[]{:S(2)}, u32[]{:S(2)}) collective-permute-start(bf16[2,64,256]{2,1,0:T(8,128)(2,1)} %get-tuple-element.8), channel_id=1, source_target_pairs={{4,0},{8,4},{12,8},{16,12},{20,16},{24,20},{28,24},{32,28},{36,32}... | collective-permute-start | bytes 196616 | tf_op jit(solution)/shard_map/ppermute | solution.py:27
  63.8 20.4 %copy-start.55 = (pred[128,27]{0,1:T(8,128)(4,1)S(1)}, pred[128,27]{0,1:T(8,128)(4,1)}, u32[]{:S(2)}) copy-start(pred[128,27]{0,1:T(8,128)(4,1)} %get-tuple-element.33) | copy-start | bytes 10372
  63.8 21.1 %copy-start.46 = (s32[128,27]{0,1:T(8,128)S(1)}, s32[128,27]{0,1:T(8,128)}, u32[]{:S(2)}) copy-start(s32[128,27]{0,1:T(8,128)} %get-tuple-element.38) | copy-start | bytes 41476
  63.8 22.1 %copy-start.54 = (pred[128,27]{0,1:T(8,128)(4,1)S(1)}, pred[128,27]{0,1:T(8,128)(4,1)}, u32[]{:S(2)}) copy-start(pred[128,27]{0,1:T(8,128)(4,1)} %get-tuple-element.34) | copy-start | bytes 10372
  63.8 23.7 %copy-start.53 = (pred[128,27]{0,1:T(8,128)(4,1)S(1)}, pred[128,27]{0,1:T(8,128)(4,1)}, u32[]{:S(2)}) copy-start(pred[128,27]{0,1:T(8,128)(4,1)} %get-tuple-element.31) | copy-start | bytes 10372
  63.8 25.0 %copy-start.41 = (pred[1024,27]{0,1:T(8,128)(4,1)S(1)}, pred[1024,27]{0,1:T(8,128)(4,1)}, u32[]{:S(2)}) copy-start(pred[1024,27]{0,1:T(8,128)(4,1)} %get-tuple-element.18) | copy-start | bytes 82948
  63.8 28.1 %copy-start.26 = (s32[1024,27]{0,1:T(8,128)S(1)}, s32[1024,27]{0,1:T(8,128)}, u32[]{:S(2)}) copy-start(s32[1024,27]{0,1:T(8,128)} %get-tuple-element.20) | copy-start | bytes 331780
  67.3 25.2 %copy-start.40 = (pred[1024,27]{0,1:T(8,128)(4,1)S(1)}, pred[1024,27]{0,1:T(8,128)(4,1)}, u32[]{:S(2)}) copy-start(pred[1024,27]{0,1:T(8,128)(4,1)} %get-tuple-element.16) | copy-start | bytes 82948
  67.3 26.1 %copy-start.25 = (s32[1024,27]{0,1:T(8,128)S(1)}, s32[1024,27]{0,1:T(8,128)}, u32[]{:S(2)}) copy-start(s32[1024,27]{0,1:T(8,128)} %get-tuple-element.19) | copy-start | bytes 331780
  67.3 27.3 %copy-start.39 = (pred[1024,27]{0,1:T(8,128)(4,1)S(1)}, pred[1024,27]{0,1:T(8,128)(4,1)}, u32[]{:S(2)}) copy-start(pred[1024,27]{0,1:T(8,128)(4,1)} %get-tuple-element.15) | copy-start | bytes 82948
  71.6 23.9 %copy-start.37 = (s32[1024,9]{0,1:T(8,128)S(1)}, s32[1024,9]{0,1:T(8,128)}, u32[]{:S(2)}) copy-start(s32[1024,9]{0,1:T(8,128)} %get-tuple-element.29) | copy-start | bytes 110596
  73.0 24.8 %copy-start.36 = (s32[1024,9]{0,1:T(8,128)S(1)}, s32[1024,9]{0,1:T(8,128)}, u32[]{:S(2)}) copy-start(s32[1024,9]{0,1:T(8,128)} %get-tuple-element.30) | copy-start | bytes 110596
  77.2 22.7 %copy-start.35 = (s32[1024,9]{0,1:T(8,128)S(1)}, s32[1024,9]{0,1:T(8,128)}, u32[]{:S(2)}) copy-start(s32[1024,9]{0,1:T(8,128)} %get-tuple-element.28) | copy-start | bytes 110596
  254.6 71.8 %copy-start.22 = (pred[1024,9]{1,0:T(8,128)(4,1)S(1)}, pred[1024,9]{1,0:T(8,128)(4,1)}, u32[]{:S(2)}) copy-start(pred[1024,9]{1,0:T(8,128)(4,1)} %copy.311) | copy-start | bytes 27652
  326.5 22.5 %slice-start.3 = ((s8[9437184]{0:T(1024)(128)(4,1)}), s8[4194304]{0:T(1024)(128)(4,1)S(1)}, s32[]{:S(2)}) async-start(s8[9437184]{0:T(1024)(128)(4,1)} %bitcast.382), calls=%async_computation.5 | async-start | bytes 8388608
  326.5 22.5 %slice-start.4 = ((s8[9437184]{0:T(1024)(128)(4,1)}), s8[4194304]{0:T(1024)(128)(4,1)S(1)}, s32[]{:S(2)}) async-start(s8[9437184]{0:T(1024)(128)(4,1)} %bitcast.382), calls=%async_computation.6 | async-start | bytes 8388608
  345.0 20.7 %slice-start = ((s8[9437184]{0:T(1024)(128)(4,1)}), s8[4194304]{0:T(1024)(128)(4,1)S(1)}, s32[]{:S(2)}) async-start(s8[9437184]{0:T(1024)(128)(4,1)} %bitcast.379), calls=%async_computation.2 | async-start | bytes 8388608
  345.0 20.7 %slice-start.1 = ((s8[9437184]{0:T(1024)(128)(4,1)}), s8[1048576]{0:T(1024)(128)(4,1)S(1)}, s32[]{:S(2)}) async-start(s8[9437184]{0:T(1024)(128)(4,1)} %bitcast.379), calls=%async_computation.3 | async-start | bytes 2097152
  387.4 20.6 %copy-start.50 = (s32[1024]{0:T(1024)S(1)}, s32[1024]{0:T(1024)}, u32[]{:S(2)}) copy-start(s32[1024]{0:T(1024)} %pad_clamp_fusion.6) | copy-start | bytes 12292
  387.4 26.9 %copy-start.31 = (s32[4096]{0:T(1024)S(1)}, s32[4096]{0:T(1024)}, u32[]{:S(2)}) copy-start(s32[4096]{0:T(1024)} %pad_clamp_fusion) | copy-start | bytes 49156
  394.0 575.7 %all-to-all-start = ((bf16[32,2,128]{2,1,0:T(2,128)(2,1)}), bf16[32,2,128]{2,1,0:T(2,128)(2,1)}, u32[]{:S(2)}, u32[]{:S(2)}) async-start(bf16[32,2,128]{2,1,0:T(2,128)(2,1)} %stack.3), calls=%async_computation | async-start | bytes 32768 | tf_op jit(solution)/shard_map/all_to_all | solution.py:13
  405.9 628.3 %all-reduce.22.cloned.1.call-start = ((), (), s32[]{:S(2)}) async-start(), calls=%async_computation.1 | async-start | bytes 1048576 | tf_op jit(solution)/shard_map/psum | solution.py:210
  927.0 23.3 %slice-start.6 = ((s8[8388608]{0:T(1024)(128)(4,1)}), s8[4194304]{0:T(1024)(128)(4,1)S(1)}, s32[]{:S(2)}) async-start(s8[8388608]{0:T(1024)(128)(4,1)} %bitcast.386), calls=%async_computation.8 | async-start | bytes 8388608
  979.1 56.3 %copy-start.2 = (f32[2,1024,256]{2,1,0:T(8,128)S(1)}, f32[2,1024,256]{2,1,0:T(8,128)}, u32[]{:S(2)}) copy-start(f32[2,1024,256]{2,1,0:T(8,128)} %param.19) | copy-start | bytes 6291460
  (61 other events, 686.6 us)
Sparse Core Ops, SparseCore 0:
  989.9 44.2 all-reduce.21
